TPU v7x, 128 devices: a whole 4x4x4 slice. The times are simulated.
128 devices in a mesh: inst: 16 (over x_lo, y, core), circ: 4 (over z), rad: 2 (over x_hi).
Axes of the slice: x: 4 (x_hi: 2, x_lo: 2; x = x_hi * 2 + x_lo), y: 4, z: 4, core: 2. Of those that a mesh axis runs over, the one named last changes fastest.
Arguments:
- flow_state: float32 [32, 6, 16, 128, 128], P('inst', None, 'rad', 'circ'), may hold values from -6 to 6
- pseudo_step: float32 [16, 128, 128], P('rad', 'circ'), may hold values from 0.04 to 0.16
- frequency: float32 [1], replicated, may hold values from 0.5 to 2
- flux_jac: float32 [3, 6, 6], replicated, may hold values from -2.5 to 2.5
- donor_offset: int32 [32], replicated, may hold values from 0 to 31, as said below
Outputs:
- new_state: float32 [32, 6, 16, 128, 128], P('inst', None, 'rad', 'circ')
Inputs may be any that keep to these rules, and one draw needn't show every extreme that they name: `donor_offset`: both 0 and 31 occur among the instances.
All inputs are finite; a program needn't handle non-finite values.
Results may differ from a plain program's by a relative error of at most 0.0003.
Values sent between devices are 32-bit elements; how exact they have to be, the bound alone decides.
A program may use at most 128 MiB of HBM per device.

v0:
```python
import functools

import jax
import jax.numpy as jnp
import numpy as np
from jax import lax
from jax.experimental import pallas as pl
from jax.experimental.pallas import tpu as pltpu
from jax.sharding import PartitionSpec as P

MESH = pl.DeviceIdType.MESH
BEND = (0.3, 0.2, 0.25)
PRODUCE = 0.4
DESTROY = 0.2
VARS = 6
TIMES = 32
LAYERS = 8
ROWS = 32
HALF = 16
LANES = 128
GROUP = 16
PAD = 8


def spectral_weights(length):
    k = np.arange(length)
    sign = np.where(k % 2 == 0, 1.0, -1.0)
    angle = np.pi * np.where(k == 0, 1, k) / length
    weights = 0.5 * sign / np.tan(angle)
    weights[0] = 0.0
    weights[length // 2] = 0.0
    return weights


def circulant(first, rows, fold):
    length = len(first)
    return [
        [first[n - m] if n >= m else fold * first[n - m + length] for m in range(length)]
        for n in range(rows)
    ]


def apply_rows(matrix, values):
    results = []
    for row in matrix:
        total = None
        for weight, value in zip(row, values):
            if abs(weight) < 1e-12:
                continue
            term = np.float32(weight) * value
            total = term if total is None else total + term
        results.append(total)
    return results


def differentiate(values):
    d = spectral_weights(TIMES)
    even = 0.5 * (d[:16] + d[16:])
    odd = 0.5 * (d[:16] - d[16:])
    even_even = 0.5 * (even[:8] + even[8:])
    even_odd = 0.5 * (even[:8] - even[8:])
    sums = [values[m] + values[m + 16] for m in range(16)]
    gaps = [values[m] - values[m + 16] for m in range(16)]
    sum_sums = [sums[m] + sums[m + 8] for m in range(8)]
    sum_gaps = [sums[m] - sums[m + 8] for m in range(8)]
    a = apply_rows(circulant(even_even, 8, 1.0), sum_sums)
    b = apply_rows(circulant(even_odd, 8, -1.0), sum_gaps)
    e = [a[n] + b[n] for n in range(8)] + [a[n] - b[n] for n in range(8)]
    o = apply_rows(circulant(odd, 16, -1.0), gaps)
    return [e[n] + o[n] for n in range(16)] + [e[n] - o[n] for n in range(16)]


def kernel(
    q, dt_hbm, freq_hbm, jac_hbm, shift_hbm, out,
    cells, step, freq, jac, shift, rows_out, rows_in, columns, ghosts,
    gathered, derived, returned, fresh,
    local_sem, out_send, out_recv, back_send, back_recv, side_send, side_recv, store_sem,
):
    me = lax.axis_index("inst")
    rad = lax.axis_index("rad")
    circ = lax.axis_index("circ")
    x, y, c = me // 8, lax.rem(me // 2, 4), lax.rem(me, 2)
    peers = []
    for dx, dy, dc in [
        (1, 2, 0), (1, 2, 1), (1, 1, 0), (1, 3, 0), (1, 1, 1), (1, 3, 1), (1, 0, 0), (1, 0, 1),
        (0, 2, 0), (0, 2, 1), (0, 1, 0), (0, 3, 0), (0, 1, 1), (0, 3, 1), (0, 0, 1),
    ]:
        peers.append((lax.rem(x + dx, 2) * 4 + lax.rem(y + dy, 4)) * 2 + lax.rem(c + dc, 2))
    after = {"circ": lax.rem(circ + 1, 4)}
    before = {"circ": lax.rem(circ + 3, 4)}
    across = {"rad": 1 - rad}

    loads = [
        pltpu.make_async_copy(
            q.at[:, :, r], cells.at[:, :, r + 1, pl.ds(PAD, ROWS)], local_sem.at[0]
        )
        for r in range(LAYERS)
    ]
    for copy in loads:
        copy.start()
    small = [
        pltpu.make_async_copy(dt_hbm, step, local_sem.at[1]),
        pltpu.make_async_copy(freq_hbm, freq, local_sem.at[2]),
        pltpu.make_async_copy(jac_hbm, jac, local_sem.at[3]),
        pltpu.make_async_copy(shift_hbm, shift, local_sem.at[4]),
        pltpu.make_async_copy(
            q.at[:, :, me // 2, pl.ds(pl.multiple_of(HALF * c, HALF), HALF)],
            gathered.at[pl.ds(2 * me, 2)], local_sem.at[5],
        ),
    ]
    for copy in small:
        copy.start()

    barrier = pltpu.get_barrier_semaphore()
    for peer in peers:
        pl.semaphore_signal(barrier, inc=1, device_id={"inst": peer}, device_id_type=MESH)
    for peer in (after, before, across):
        pl.semaphore_signal(barrier, inc=1, device_id=peer, device_id_type=MESH)
    pl.semaphore_wait(barrier, GROUP - 1 + 3)

    def send_out(v, _):
        for peer in peers:
            pltpu.make_async_remote_copy(
                q.at[:, pl.ds(v, 1), peer // 2, pl.ds(pl.multiple_of(HALF * lax.rem(peer, 2), HALF), HALF)],
                gathered.at[pl.ds(2 * me, 2), pl.ds(v, 1)],
                out_send, out_recv.at[v],
                device_id={"inst": peer}, device_id_type=MESH,
            ).start()
        return 0

    lax.fori_loop(0, VARS, send_out, 0)
    layer_copy = pltpu.make_async_remote_copy(
        q.at[:, :, (LAYERS - 1) * (1 - rad)],
        cells.at[:, :, (LAYERS + 1) * rad, pl.ds(PAD, ROWS)],
        side_send.at[0], side_recv.at[0], device_id=across, device_id_type=MESH,
    )
    layer_copy.start()

    for copy in loads:
        copy.wait()

    lane = lax.broadcasted_iota(jnp.int32, (ROWS, LANES), 1)

    def pack(n, _):
        packed = jnp.zeros((ROWS, LANES), jnp.float32)
        for v in range(VARS):
            for r in range(LAYERS):
                rows_out[0, n, v, r:r + 1] = cells[n, v, r + 1, PAD + ROWS - 1:PAD + ROWS]
                rows_out[1, n, v, r:r + 1] = cells[n, v, r + 1, PAD:PAD + 1]
                j = v * LAYERS + r
                block = pltpu.roll(cells[n, v, r + 1, PAD:PAD + ROWS], (2 * j - 63) % LANES, 1)
                packed = jnp.where(lane // 2 == j, block, packed)
        columns[n, ROWS:2 * ROWS] = packed
        return 0

    lax.fori_loop(0, 2, pack, 0)
    side_copies = [
        pltpu.make_async_remote_copy(
            rows_out.at[0], rows_in.at[0], side_send.at[1], side_recv.at[1],
            device_id=after, device_id_type=MESH,
        ),
        pltpu.make_async_remote_copy(
            rows_out.at[1], rows_in.at[1], side_send.at[2], side_recv.at[2],
            device_id=before, device_id_type=MESH,
        ),
        pltpu.make_async_remote_copy(
            columns.at[:, pl.ds(ROWS, ROWS)], columns.at[:, pl.ds(0, ROWS)],
            side_send.at[3], side_recv.at[3], device_id=after, device_id_type=MESH,
        ),
        pltpu.make_async_remote_copy(
            columns.at[:, pl.ds(ROWS, ROWS)], columns.at[:, pl.ds(2 * ROWS, ROWS)],
            side_send.at[4], side_recv.at[4], device_id=before, device_id_type=MESH,
        ),
    ]
    for copy in side_copies:
        copy.start()
    cells[:, :, (LAYERS + 1) * rad, PAD:PAD + ROWS] = jnp.zeros((2, VARS, ROWS, LANES), jnp.float32)
    for copy in small:
        copy.wait()
    for copy in side_copies:
        copy.wait_recv()

    def unpack(n, _):
        for v in range(VARS):
            for r in range(LAYERS):
                cells[n, v, r + 1, PAD - 1:PAD] = rows_in[0, n, v, r:r + 1]
                cells[n, v, r + 1, PAD + ROWS:PAD + ROWS + 1] = rows_in[1, n, v, r:r + 1]
        s = shift[2 * me + n]
        stator = columns[n, pl.ds(ROWS + s, ROWS)]
        rotor = columns[n, pl.ds(ROWS - s, ROWS)]
        ghosts[n] = jnp.where(lane % 2 == 0, pltpu.roll(rotor, LANES - 1, 1), pltpu.roll(stator, 1, 1))
        return 0

    lax.fori_loop(0, 2, unpack, 0)
    layer_copy.wait_recv()

    def spatial(t, _):
        n, r = t // LAYERS, lax.rem(t, LAYERS)
        ghost = ghosts[n]
        here, sides = [], [[], [], []]
        for v in range(VARS):
            now = cells[n, v, r + 1, PAD:PAD + ROWS]
            here.append(now)
            sides[0].append((cells[n, v, r, PAD:PAD + ROWS], cells[n, v, r + 2, PAD:PAD + ROWS]))
            sides[1].append((cells[n, v, r + 1, PAD - 1:PAD + ROWS - 1], cells[n, v, r + 1, PAD + 1:PAD + ROWS + 1]))
            first = 63 - 2 * LAYERS * v
            placed = pltpu.roll(ghost, (first if first > 2 * LAYERS - 2 else first + LANES) - 2 * r, 1)
            lower = jnp.where(lane == 64, placed, jnp.where(lane == 0, 0.0, pltpu.roll(now, 1, 1)))
            upper = jnp.where(lane == 63, placed, jnp.where(lane == LANES - 1, 0.0, pltpu.roll(now, LANES - 1, 1)))
            sides[2].append((lower, upper))
        linear = [None] * VARS
        rest = [3.0 * now for now in here]
        for d in range(3):
            low0 = (0.25 * BEND[d]) * sides[d][0][0] + 0.5
            high0 = (0.25 * BEND[d]) * sides[d][0][1] - 0.5
            for v in range(VARS):
                low, high = sides[d][v]
                rest[v] = rest[v] + (high * high0 - low * low0)
                gap = high - low
                for u in range(VARS):
                    term = jac[d, u, v] * gap
                    linear[u] = term if linear[u] is None else linear[u] + term
        eddy = here[5]
        source = PRODUCE * eddy * jnp.sqrt(1.0 + here[1] * here[1] + here[2] * here[2]) - DESTROY * eddy * jnp.abs(eddy)
        rest[5] = rest[5] - source
        pace = step[r]
        for v in range(VARS):
            fresh[n, v, r] = here[v] - pace * (rest[v] + 0.5 * linear[v])
        return 0

    lax.fori_loop(0, 2 * LAYERS, spatial, 0)

    def send_back(v, _):
        part = gathered.at[pl.ds(0, TIMES - 2), pl.ds(v, 1)]
        pltpu.make_async_copy(part, part, out_recv.at[v]).wait()
        for h in range(HALF // 8):
            values = [gathered[m, v, 8 * h:8 * h + 8] for m in range(TIMES)]
            for m, value in enumerate(differentiate(values)):
                derived[m, v, 8 * h:8 * h + 8] = value
        for peer in peers:
            pltpu.make_async_remote_copy(
                derived.at[pl.ds(2 * peer, 2), pl.ds(v, 1)],
                returned.at[:, pl.ds(v, 1), me // 2, pl.ds(pl.multiple_of(HALF * c, HALF), HALF)],
                back_send, back_recv.at[v],
                device_id={"inst": peer}, device_id_type=MESH,
            ).start()
        for i in range(2):
            returned[i, v, me // 2, pl.ds(pl.multiple_of(HALF * c, HALF), HALF)] = derived[2 * me + i, v]
        return 0

    lax.fori_loop(0, VARS, send_back, 0)

    def finish(v, _):
        part = gathered.at[pl.ds(0, TIMES - 2), pl.ds(v, 1)]
        pltpu.make_async_copy(part, part, back_recv.at[v]).wait()
        pace = freq[0]
        for r in range(LAYERS):
            scaled = pace * step[r]
            for n in range(2):
                fresh[n, v, r] = fresh[n, v, r] - scaled * returned[n, v, r]
        pltpu.make_async_copy(fresh.at[:, pl.ds(v, 1)], out.at[:, pl.ds(v, 1)], store_sem).start()
        return 0

    lax.fori_loop(0, VARS, finish, 0)
    pltpu.make_async_copy(fresh, out, store_sem).wait()
    whole = gathered.at[pl.ds(0, TIMES - 2)]
    pltpu.make_async_copy(whole, whole, out_send).wait()
    pltpu.make_async_copy(whole, whole, back_send).wait()
    layer_copy.wait_send()
    for copy in side_copies:
        copy.wait_send()


def per_device(flow_state, pseudo_step, frequency, flux_jac, donor_offset):
    f32 = jnp.float32
    anywhere = pl.BlockSpec(memory_space=pl.ANY)
    in_hbm = pl.BlockSpec(memory_space=pltpu.HBM)
    dma = pltpu.SemaphoreType.DMA
    return pl.pallas_call(
        kernel,
        name="pseudo_time_step",
        out_shape=jax.ShapeDtypeStruct(flow_state.shape, f32),
        in_specs=[in_hbm] * 5,
        out_specs=anywhere,
        scratch_shapes=[
            pltpu.VMEM((2, VARS, LAYERS + 2, ROWS + 2 * PAD, LANES), f32),
            pltpu.VMEM((LAYERS, ROWS, LANES), f32),
            pltpu.SMEM((1,), f32),
            pltpu.SMEM((3, VARS, VARS), f32),
            pltpu.SMEM((TIMES,), jnp.int32),
            pltpu.VMEM((2, 2, VARS, LAYERS, LANES), f32),
            pltpu.VMEM((2, 2, VARS, LAYERS, LANES), f32),
            pltpu.VMEM((2, 3 * ROWS, LANES), f32),
            pltpu.VMEM((2, ROWS, LANES), f32),
            pltpu.VMEM((TIMES, VARS, HALF, LANES), f32),
            pltpu.VMEM((TIMES, VARS, HALF, LANES), f32),
            pltpu.VMEM((2, VARS, LAYERS, ROWS, LANES), f32),
            pltpu.VMEM((2, VARS, LAYERS, ROWS, LANES), f32),
            dma((6,)), dma, dma((VARS,)), dma, dma((VARS,)), dma((5,)), dma((5,)), dma,
        ],
        compiler_params=pltpu.CompilerParams(
            collective_id=0, has_side_effects=True, vmem_limit_bytes=60 << 20
        ),
        cost_estimate=pl.CostEstimate(flops=40_000_000, bytes_accessed=4_000_000, transcendentals=0),
    )(flow_state, pseudo_step, frequency, flux_jac, donor_offset)


def solution(mesh):
    return jax.shard_map(
        per_device,
        mesh=mesh,
        in_specs=(P("inst", None, "rad", "circ", None), P("rad", "circ", None), P(), P(), P()),
        out_specs=P("inst", None, "rad", "circ", None),
        check_vma=False,
    )
```

profile of v0, /device:TPU:1, one launch (start us, length us, event | category | flops | bytes accessed | tf_op | source)
XLA Modules:
  0.0 58.1 jit_solution(5285183882435347163)
XLA Ops:
  0.7 54.8 %pseudo_time_step.1 = f32[2,6,8,32,128]{4,3,2,1,0:T(8,128)} custom-call(f32[2,6,8,32,128]{4,3,2,1,0:T(8,128)} %q.1, f32[8,32,128]{2,1,0:T(8,128)} %dt_hbm.1, f32[1]{0:T(128)S(6)} %copy.7.freq_hbm, f32[3,6,6]{2,1,0:T(8,128)} %jac_hbm.1, s32[32]{0:T(128)} %shift_hbm.1), custom_call_target="tpu_custom_call" | custom-call | flops 40000000 | bytes 4000000 | tf_op jit(solution)/shard_map/pseudo_time_step/pallas_call | solution.py:279
  55.5 2.7 %copy.8 = f32[2,6,8,32,128]{4,3,2,1,0:T(8,128)} copy(f32[2,6,8,32,128]{4,3,2,1,0:T(8,128)} %pseudo_time_step.1) | data formatting | bytes 3145728
where the time goes:
time: 58.3 us; the launch traced here: 58.1 us
  Pallas kernels  54.8 us (94%)
  local copies, waits for them, and re-layouts  2.67 us (5%)
  between operations  0.66 us (1%)
    pallas_call x1, Pallas kernels, per_device(): pl.pallas_call(kernel, name='pseudo_time_step', out_shape=jax.ShapeDtypeS...  54.8 us
    unnamed x1, local copies, waits for them, and re-layouts  2.67 us

commit v1 on v0

--- a/solution.py
+++ b/solution.py
@@ -71,10 +71,10 @@
 
 
 def kernel(
-    q, dt_hbm, freq_hbm, jac_hbm, shift_hbm, out,
-    cells, step, freq, jac, shift, rows_out, rows_in, columns, ghosts,
+    q, dt_hbm, freq, jac_hbm, shift_hbm, out,
+    cells, step, jac, shift, rows_out, rows_in, columns, ghosts,
     gathered, derived, returned, fresh,
-    local_sem, out_send, out_recv, back_send, back_recv, side_send, side_recv, store_sem,
+    local_sem, out_send, out_recv, back_send, back_recv, side_send, side_recv,
 ):
     me = lax.axis_index("inst")
     rad = lax.axis_index("rad")
@@ -100,7 +100,6 @@
         copy.start()
     small = [
         pltpu.make_async_copy(dt_hbm, step, local_sem.at[1]),
-        pltpu.make_async_copy(freq_hbm, freq, local_sem.at[2]),
         pltpu.make_async_copy(jac_hbm, jac, local_sem.at[3]),
         pltpu.make_async_copy(shift_hbm, shift, local_sem.at[4]),
         pltpu.make_async_copy(
@@ -177,6 +176,27 @@
     cells[:, :, (LAYERS + 1) * rad, PAD:PAD + ROWS] = jnp.zeros((2, VARS, ROWS, LANES), jnp.float32)
     for copy in small:
         copy.wait()
+
+    def send_back(v, _):
+        part = gathered.at[pl.ds(0, TIMES - 2), pl.ds(v, 1)]
+        pltpu.make_async_copy(part, part, out_recv.at[v]).wait()
+        for h in range(HALF // 8):
+            values = [gathered[m, v, 8 * h:8 * h + 8] for m in range(TIMES)]
+            for m, value in enumerate(differentiate(values)):
+                derived[m, v, 8 * h:8 * h + 8] = value
+        for peer in peers:
+            pltpu.make_async_remote_copy(
+                derived.at[pl.ds(2 * peer, 2), pl.ds(v, 1)],
+                returned.at[:, pl.ds(v, 1), me // 2, pl.ds(pl.multiple_of(HALF * c, HALF), HALF)],
+                back_send, back_recv.at[v],
+                device_id={"inst": peer}, device_id_type=MESH,
+            ).start()
+        for i in range(2):
+            returned[i, v, me // 2, pl.ds(pl.multiple_of(HALF * c, HALF), HALF)] = derived[2 * me + i, v]
+        return 0
+
+    lax.fori_loop(0, VARS, send_back, 0)
+
     for copy in side_copies:
         copy.wait_recv()
 
@@ -230,26 +250,6 @@
 
     lax.fori_loop(0, 2 * LAYERS, spatial, 0)
 
-    def send_back(v, _):
-        part = gathered.at[pl.ds(0, TIMES - 2), pl.ds(v, 1)]
-        pltpu.make_async_copy(part, part, out_recv.at[v]).wait()
-        for h in range(HALF // 8):
-            values = [gathered[m, v, 8 * h:8 * h + 8] for m in range(TIMES)]
-            for m, value in enumerate(differentiate(values)):
-                derived[m, v, 8 * h:8 * h + 8] = value
-        for peer in peers:
-            pltpu.make_async_remote_copy(
-                derived.at[pl.ds(2 * peer, 2), pl.ds(v, 1)],
-                returned.at[:, pl.ds(v, 1), me // 2, pl.ds(pl.multiple_of(HALF * c, HALF), HALF)],
-                back_send, back_recv.at[v],
-                device_id={"inst": peer}, device_id_type=MESH,
-            ).start()
-        for i in range(2):
-            returned[i, v, me // 2, pl.ds(pl.multiple_of(HALF * c, HALF), HALF)] = derived[2 * me + i, v]
-        return 0
-
-    lax.fori_loop(0, VARS, send_back, 0)
-
     def finish(v, _):
         part = gathered.at[pl.ds(0, TIMES - 2), pl.ds(v, 1)]
         pltpu.make_async_copy(part, part, back_recv.at[v]).wait()
@@ -257,12 +257,10 @@
         for r in range(LAYERS):
             scaled = pace * step[r]
             for n in range(2):
-                fresh[n, v, r] = fresh[n, v, r] - scaled * returned[n, v, r]
-        pltpu.make_async_copy(fresh.at[:, pl.ds(v, 1)], out.at[:, pl.ds(v, 1)], store_sem).start()
+                out[n, v, r] = fresh[n, v, r] - scaled * returned[n, v, r]
         return 0
 
     lax.fori_loop(0, VARS, finish, 0)
-    pltpu.make_async_copy(fresh, out, store_sem).wait()
     whole = gathered.at[pl.ds(0, TIMES - 2)]
     pltpu.make_async_copy(whole, whole, out_send).wait()
     pltpu.make_async_copy(whole, whole, back_send).wait()
@@ -274,18 +272,18 @@
 def per_device(flow_state, pseudo_step, frequency, flux_jac, donor_offset):
     f32 = jnp.float32
     anywhere = pl.BlockSpec(memory_space=pl.ANY)
-    in_hbm = pl.BlockSpec(memory_space=pltpu.HBM)
+    scalar = pl.BlockSpec(memory_space=pltpu.SMEM)
+    hbm = functools.partial(pltpu.with_memory_space_constraint, memory_space=pltpu.HBM)
     dma = pltpu.SemaphoreType.DMA
     return pl.pallas_call(
         kernel,
         name="pseudo_time_step",
-        out_shape=jax.ShapeDtypeStruct(flow_state.shape, f32),
-        in_specs=[in_hbm] * 5,
-        out_specs=anywhere,
+        out_shape=pltpu.VMEM(flow_state.shape, f32),
+        in_specs=[anywhere, anywhere, scalar, anywhere, anywhere],
+        out_specs=pl.BlockSpec(memory_space=pltpu.VMEM),
         scratch_shapes=[
             pltpu.VMEM((2, VARS, LAYERS + 2, ROWS + 2 * PAD, LANES), f32),
             pltpu.VMEM((LAYERS, ROWS, LANES), f32),
-            pltpu.SMEM((1,), f32),
             pltpu.SMEM((3, VARS, VARS), f32),
             pltpu.SMEM((TIMES,), jnp.int32),
             pltpu.VMEM((2, 2, VARS, LAYERS, LANES), f32),
@@ -296,13 +294,13 @@
             pltpu.VMEM((TIMES, VARS, HALF, LANES), f32),
             pltpu.VMEM((2, VARS, LAYERS, ROWS, LANES), f32),
             pltpu.VMEM((2, VARS, LAYERS, ROWS, LANES), f32),
-            dma((6,)), dma, dma((VARS,)), dma, dma((VARS,)), dma((5,)), dma((5,)), dma,
+            dma((6,)), dma, dma((VARS,)), dma, dma((VARS,)), dma((5,)), dma((5,)),
         ],
         compiler_params=pltpu.CompilerParams(
-            collective_id=0, has_side_effects=True, vmem_limit_bytes=60 << 20
+            collective_id=0, has_side_effects=True, vmem_limit_bytes=40 << 20
         ),
         cost_estimate=pl.CostEstimate(flops=40_000_000, bytes_accessed=4_000_000, transcendentals=0),
-    )(flow_state, pseudo_step, frequency, flux_jac, donor_offset)
+    )(hbm(flow_state), hbm(pseudo_step), frequency, hbm(flux_jac), hbm(donor_offset))
 
 
 def solution(mesh):

time: 58.3 us -> 49.3 us (0.85)
  Pallas kernels: 54.8 us -> 47.4 us
  local copies, waits for them, and re-layouts: 2.67 us -> 1.15 us
    pallas_call x1, Pallas kernels: 54.8 us -> 47.4 us  [per_device(): pl.pallas_call(kernel, name='pseudo_time_step', out_shape=pltpu.VMEM(flow...]
    unnamed x1, local copies, waits for them, and re-layouts: 2.67 us -> 1.15 us
where the time goes in v1:
time: 49.3 us; the launch traced here: 49.2 us
  Pallas kernels  47.4 us (96%)
  local copies, waits for them, and re-layouts  1.15 us (2%)
  between operations  0.66 us (1%)
    pallas_call x1, Pallas kernels, per_device(): pl.pallas_call(kernel, name='pseudo_time_step', out_shape=pltpu.VMEM(flow...  47.4 us
    unnamed x1, local copies, waits for them, and re-layouts  1.15 us

profile of v1, /device:TPU:1, one launch (start us, length us, event | category | flops | bytes accessed | tf_op | source)
XLA Modules:
  0.0 49.2 jit_solution(1116387541680701895)
XLA Ops:
  0.7 47.4 %pseudo_time_step.1 = f32[2,6,8,32,128]{4,3,2,1,0:T(8,128)S(1)} custom-call(f32[2,6,8,32,128]{4,3,2,1,0:T(8,128)} %q.1, f32[8,32,128]{2,1,0:T(8,128)} %dt_hbm.1, f32[1]{0:T(128)S(6)} %copy.8.freq, f32[3,6,6]{2,1,0:T(8,128)} %jac_hbm.1, s32[32]{0:T(128)} %shift_hbm.1), custom_call_target="tpu_custom_call" | custom-call | flops 40000000 | bytes 4000000 | tf_op jit(solution)/shard_map/pseudo_time_step/pallas_call | solution.py:278
  48.1 1.1 %copy.7 = f32[2,6,8,32,128]{4,3,2,1,0:T(8,128)} copy(f32[2,6,8,32,128]{4,3,2,1,0:T(8,128)S(1)} %pseudo_time_step.1) | data formatting | bytes 3145728

commit v2 on v1

--- a/solution.py
+++ b/solution.py
@@ -16,7 +16,9 @@
 TIMES = 32
 LAYERS = 8
 ROWS = 32
-HALF = 16
+TILE = 8
+TAKE = 2
+GROUPS = VARS // TAKE
 LANES = 128
 GROUP = 16
 PAD = 8
@@ -73,8 +75,8 @@
 def kernel(
     q, dt_hbm, freq, jac_hbm, shift_hbm, out,
     cells, step, jac, shift, rows_out, rows_in, columns, ghosts,
-    gathered, derived, returned, fresh,
-    local_sem, out_send, out_recv, back_send, back_recv, side_send, side_recv,
+    gathered, beyond, derived, returned, fresh,
+    local_sem, out_send, out_recv, back_send, back_recv, side_send, side_recv, swap_send, swap_recv,
 ):
     me = lax.axis_index("inst")
     rad = lax.axis_index("rad")
@@ -85,11 +87,20 @@
         (1, 2, 0), (1, 2, 1), (1, 1, 0), (1, 3, 0), (1, 1, 1), (1, 3, 1), (1, 0, 0), (1, 0, 1),
         (0, 2, 0), (0, 2, 1), (0, 1, 0), (0, 3, 0), (0, 1, 1), (0, 3, 1), (0, 0, 1),
     ]:
-        peers.append((lax.rem(x + dx, 2) * 4 + lax.rem(y + dy, 4)) * 2 + lax.rem(c + dc, 2))
+        px, py, pc = lax.rem(x + dx, 2), lax.rem(y + dy, 4), lax.rem(c + dc, 2)
+        peers.append(((px * 4 + py) * 2 + pc, px * 4 + pc * 2, pl.multiple_of(py * TILE, TILE)))
     after = {"circ": lax.rem(circ + 1, 4)}
     before = {"circ": lax.rem(circ + 3, 4)}
-    across = {"rad": 1 - rad}
-
+    across = {"rad": 1 - rad, "inst": ((1 - x) * 4 + y) * 2 + 1 - c}
+    meets = jnp.logical_and(x == 1 - rad, c == 1 - rad)
+
+    barrier = pltpu.get_barrier_semaphore()
+    for peer, _, _ in peers:
+        pl.semaphore_signal(barrier, inc=1, device_id={"inst": peer}, device_id_type=MESH)
+    for peer in (after, before, across):
+        pl.semaphore_signal(barrier, inc=1, device_id=peer, device_id_type=MESH)
+
+    my_layer, my_row = x * 4 + c * 2, pl.multiple_of(y * TILE, TILE)
     loads = [
         pltpu.make_async_copy(
             q.at[:, :, r], cells.at[:, :, r + 1, pl.ds(PAD, ROWS)], local_sem.at[0]
@@ -100,40 +111,32 @@
         copy.start()
     small = [
         pltpu.make_async_copy(dt_hbm, step, local_sem.at[1]),
-        pltpu.make_async_copy(jac_hbm, jac, local_sem.at[3]),
-        pltpu.make_async_copy(shift_hbm, shift, local_sem.at[4]),
-        pltpu.make_async_copy(
-            q.at[:, :, me // 2, pl.ds(pl.multiple_of(HALF * c, HALF), HALF)],
-            gathered.at[pl.ds(2 * me, 2)], local_sem.at[5],
-        ),
-    ]
+        pltpu.make_async_copy(jac_hbm, jac, local_sem.at[2]),
+        pltpu.make_async_copy(shift_hbm, shift, local_sem.at[3]),
+    ]
+    for slot in range(2):
+        small.append(
+            pltpu.make_async_copy(
+                q.at[:, :, my_layer + lax.rem(slot + 1 - rad, 2), pl.ds(my_row, TILE)],
+                gathered.at[slot, pl.ds(2 * me, 2)], local_sem.at[4 + slot],
+            )
+        )
     for copy in small:
         copy.start()
-
-    barrier = pltpu.get_barrier_semaphore()
-    for peer in peers:
-        pl.semaphore_signal(barrier, inc=1, device_id={"inst": peer}, device_id_type=MESH)
-    for peer in (after, before, across):
-        pl.semaphore_signal(barrier, inc=1, device_id=peer, device_id_type=MESH)
     pl.semaphore_wait(barrier, GROUP - 1 + 3)
 
-    def send_out(v, _):
-        for peer in peers:
+    def send_out(k, _):
+        slot, g = k // GROUPS, lax.rem(k, GROUPS)
+        for peer, layer, row in peers:
             pltpu.make_async_remote_copy(
-                q.at[:, pl.ds(v, 1), peer // 2, pl.ds(pl.multiple_of(HALF * lax.rem(peer, 2), HALF), HALF)],
-                gathered.at[pl.ds(2 * me, 2), pl.ds(v, 1)],
-                out_send, out_recv.at[v],
+                q.at[:, pl.ds(g * TAKE, TAKE), layer + lax.rem(slot + 1 - rad, 2), pl.ds(row, TILE)],
+                gathered.at[slot, pl.ds(2 * me, 2), pl.ds(g * TAKE, TAKE)],
+                out_send, out_recv.at[k],
                 device_id={"inst": peer}, device_id_type=MESH,
             ).start()
         return 0
 
-    lax.fori_loop(0, VARS, send_out, 0)
-    layer_copy = pltpu.make_async_remote_copy(
-        q.at[:, :, (LAYERS - 1) * (1 - rad)],
-        cells.at[:, :, (LAYERS + 1) * rad, pl.ds(PAD, ROWS)],
-        side_send.at[0], side_recv.at[0], device_id=across, device_id_type=MESH,
-    )
-    layer_copy.start()
+    lax.fori_loop(0, 2 * GROUPS, send_out, 0)
 
     for copy in loads:
         copy.wait()
@@ -155,47 +158,103 @@
     lax.fori_loop(0, 2, pack, 0)
     side_copies = [
         pltpu.make_async_remote_copy(
-            rows_out.at[0], rows_in.at[0], side_send.at[1], side_recv.at[1],
+            rows_out.at[0], rows_in.at[0], side_send.at[0], side_recv.at[0],
             device_id=after, device_id_type=MESH,
         ),
         pltpu.make_async_remote_copy(
-            rows_out.at[1], rows_in.at[1], side_send.at[2], side_recv.at[2],
+            rows_out.at[1], rows_in.at[1], side_send.at[1], side_recv.at[1],
             device_id=before, device_id_type=MESH,
         ),
         pltpu.make_async_remote_copy(
             columns.at[:, pl.ds(ROWS, ROWS)], columns.at[:, pl.ds(0, ROWS)],
-            side_send.at[3], side_recv.at[3], device_id=after, device_id_type=MESH,
+            side_send.at[2], side_recv.at[2], device_id=after, device_id_type=MESH,
         ),
         pltpu.make_async_remote_copy(
             columns.at[:, pl.ds(ROWS, ROWS)], columns.at[:, pl.ds(2 * ROWS, ROWS)],
-            side_send.at[4], side_recv.at[4], device_id=before, device_id_type=MESH,
+            side_send.at[3], side_recv.at[3], device_id=before, device_id_type=MESH,
         ),
     ]
     for copy in side_copies:
         copy.start()
-    cells[:, :, (LAYERS + 1) * rad, PAD:PAD + ROWS] = jnp.zeros((2, VARS, ROWS, LANES), jnp.float32)
+    cells[:, :, 0, PAD:PAD + ROWS] = jnp.zeros((2, VARS, ROWS, LANES), jnp.float32)
+    cells[:, :, LAYERS + 1, PAD:PAD + ROWS] = jnp.zeros((2, VARS, ROWS, LANES), jnp.float32)
     for copy in small:
         copy.wait()
 
-    def send_back(v, _):
-        part = gathered.at[pl.ds(0, TIMES - 2), pl.ds(v, 1)]
-        pltpu.make_async_copy(part, part, out_recv.at[v]).wait()
-        for h in range(HALF // 8):
-            values = [gathered[m, v, 8 * h:8 * h + 8] for m in range(TIMES)]
+    def wait_part(sem):
+        part = gathered.at[0, pl.ds(0, TIMES - 2), pl.ds(0, TAKE)]
+        pltpu.make_async_copy(part, part, sem).wait()
+
+    swaps = [
+        pltpu.make_async_remote_copy(
+            gathered.at[0, :, pl.ds(g * TAKE, TAKE)], beyond.at[:, pl.ds(g * TAKE, TAKE)],
+            swap_send.at[g], swap_recv.at[g], device_id=across, device_id_type=MESH,
+        )
+        for g in range(GROUPS)
+    ]
+
+    @pl.when(meets)
+    def _():
+        for g in range(GROUPS):
+            wait_part(out_recv.at[g])
+            swaps[g].start()
+
+    pace = freq[0]
+    side = (1 - 2 * rad).astype(jnp.float32)
+
+    def radial_term(m, _):
+        w = [beyond[m, v] for v in range(VARS)]
+        curved = (0.25 * BEND[0]) * w[0]
+        for u in range(VARS):
+            total = curved * w[u]
+            for v in range(VARS):
+                total = total + (0.5 * jac[0, u, v]) * w[v]
+            beyond[m, u] = side * total - 0.5 * w[u]
+        return 0
+
+    def send_back(k, _):
+        slot = lax.rem(k // GROUPS + meets.astype(jnp.int32), 2)
+        g = lax.rem(k, GROUPS)
+        meeting = jnp.logical_and(meets, slot == 0)
+
+        @pl.when(jnp.logical_not(meeting))
+        def _():
+            wait_part(out_recv.at[slot * GROUPS + g])
+
+        @pl.when(jnp.logical_and(meeting, g == 0))
+        def _():
+            for swap in swaps:
+                swap.wait_recv()
+            lax.fori_loop(0, TIMES, radial_term, 0)
+
+        for i in range(TAKE):
+            v = g * TAKE + i
+            values = [gathered[slot, m, v] for m in range(TIMES)]
             for m, value in enumerate(differentiate(values)):
-                derived[m, v, 8 * h:8 * h + 8] = value
-        for peer in peers:
+                derived[slot, m, v] = pace * value
+
+        @pl.when(meeting)
+        def _():
+            for i in range(TAKE):
+                v = g * TAKE + i
+                for m in range(TIMES):
+                    derived[0, m, v] = derived[0, m, v] + beyond[m, v]
+
+        layer = my_layer + lax.rem(slot + 1 - rad, 2)
+        for peer, _, _ in peers:
             pltpu.make_async_remote_copy(
-                derived.at[pl.ds(2 * peer, 2), pl.ds(v, 1)],
-                returned.at[:, pl.ds(v, 1), me // 2, pl.ds(pl.multiple_of(HALF * c, HALF), HALF)],
-                back_send, back_recv.at[v],
+                derived.at[slot, pl.ds(2 * peer, 2), pl.ds(g * TAKE, TAKE)],
+                returned.at[:, pl.ds(g * TAKE, TAKE), layer, pl.ds(my_row, TILE)],
+                back_send, back_recv.at[slot * GROUPS + g],
                 device_id={"inst": peer}, device_id_type=MESH,
             ).start()
-        for i in range(2):
-            returned[i, v, me // 2, pl.ds(pl.multiple_of(HALF * c, HALF), HALF)] = derived[2 * me + i, v]
-        return 0
-
-    lax.fori_loop(0, VARS, send_back, 0)
+        for n in range(2):
+            for i in range(TAKE):
+                v = g * TAKE + i
+                returned[n, v, layer, pl.ds(my_row, TILE)] = derived[slot, 2 * me + n, v]
+        return 0
+
+    lax.fori_loop(0, 2 * GROUPS, send_back, 0)
 
     for copy in side_copies:
         copy.wait_recv()
@@ -212,7 +271,6 @@
         return 0
 
     lax.fori_loop(0, 2, unpack, 0)
-    layer_copy.wait_recv()
 
     def spatial(t, _):
         n, r = t // LAYERS, lax.rem(t, LAYERS)
@@ -250,23 +308,29 @@
 
     lax.fori_loop(0, 2 * LAYERS, spatial, 0)
 
-    def finish(v, _):
-        part = gathered.at[pl.ds(0, TIMES - 2), pl.ds(v, 1)]
-        pltpu.make_async_copy(part, part, back_recv.at[v]).wait()
-        pace = freq[0]
-        for r in range(LAYERS):
-            scaled = pace * step[r]
+    def finish(k, _):
+        slot, g = 1 - k // GROUPS, lax.rem(k, GROUPS)
+        wait_part(back_recv.at[slot * GROUPS + g])
+        for pair in range(LAYERS // 2):
+            r = 2 * pair + lax.rem(slot + 1 - rad, 2)
+            scaled = step[r]
             for n in range(2):
-                out[n, v, r] = fresh[n, v, r] - scaled * returned[n, v, r]
-        return 0
-
-    lax.fori_loop(0, VARS, finish, 0)
-    whole = gathered.at[pl.ds(0, TIMES - 2)]
+                for i in range(TAKE):
+                    v = g * TAKE + i
+                    out[n, v, r] = fresh[n, v, r] - scaled * returned[n, v, r]
+        return 0
+
+    lax.fori_loop(0, 2 * GROUPS, finish, 0)
+    whole = gathered.at[:, pl.ds(0, TIMES - 2)]
     pltpu.make_async_copy(whole, whole, out_send).wait()
     pltpu.make_async_copy(whole, whole, back_send).wait()
-    layer_copy.wait_send()
     for copy in side_copies:
         copy.wait_send()
+
+    @pl.when(meets)
+    def _():
+        for swap in swaps:
+            swap.wait_send()
 
 
 def per_device(flow_state, pseudo_step, frequency, flux_jac, donor_offset):
@@ -290,11 +354,13 @@
             pltpu.VMEM((2, 2, VARS, LAYERS, LANES), f32),
             pltpu.VMEM((2, 3 * ROWS, LANES), f32),
             pltpu.VMEM((2, ROWS, LANES), f32),
-            pltpu.VMEM((TIMES, VARS, HALF, LANES), f32),
-            pltpu.VMEM((TIMES, VARS, HALF, LANES), f32),
+            pltpu.VMEM((2, TIMES, VARS, TILE, LANES), f32),
+            pltpu.VMEM((TIMES, VARS, TILE, LANES), f32),
+            pltpu.VMEM((2, TIMES, VARS, TILE, LANES), f32),
             pltpu.VMEM((2, VARS, LAYERS, ROWS, LANES), f32),
             pltpu.VMEM((2, VARS, LAYERS, ROWS, LANES), f32),
-            dma((6,)), dma, dma((VARS,)), dma, dma((VARS,)), dma((5,)), dma((5,)),
+            dma((6,)), dma, dma((2 * GROUPS,)), dma, dma((2 * GROUPS,)),
+            dma((4,)), dma((4,)), dma((GROUPS,)), dma((GROUPS,)),
         ],
         compiler_params=pltpu.CompilerParams(
             collective_id=0, has_side_effects=True, vmem_limit_bytes=40 << 20

time: 49.3 us -> 45.3 us (0.919)
  Pallas kernels: 47.4 us -> 43.4 us
    pallas_call x1, Pallas kernels: 47.4 us -> 43.4 us  [per_device(): pl.pallas_call(kernel, name='pseudo_time_step', out_shape=pltpu.VMEM(flow...]
where the time goes in v2:
time: 45.3 us; the launch traced here: 45.2 us
  Pallas kernels  43.4 us (96%)
  local copies, waits for them, and re-layouts  1.15 us (3%)
  between operations  0.66 us (1%)
    pallas_call x1, Pallas kernels, per_device(): pl.pallas_call(kernel, name='pseudo_time_step', out_shape=pltpu.VMEM(flow...  43.4 us
    unnamed x1, local copies, waits for them, and re-layouts  1.15 us

profile of v2, /device:TPU:1, one launch (start us, length us, event | category | flops | bytes accessed | tf_op | source)
XLA Modules:
  0.0 45.2 jit_solution(12847111167395183380)
XLA Ops:
  0.7 43.4 %pseudo_time_step.1 = f32[2,6,8,32,128]{4,3,2,1,0:T(8,128)S(1)} custom-call(f32[2,6,8,32,128]{4,3,2,1,0:T(8,128)} %q.1, f32[8,32,128]{2,1,0:T(8,128)} %dt_hbm.1, f32[1]{0:T(128)S(6)} %copy.8.freq, f32[3,6,6]{2,1,0:T(8,128)} %jac_hbm.1, s32[32]{0:T(128)} %shift_hbm.1), custom_call_target="tpu_custom_call" | custom-call | flops 40000000 | bytes 4000000 | tf_op jit(solution)/shard_map/pseudo_time_step/pallas_call | solution.py:342
  44.0 1.1 %copy.7 = f32[2,6,8,32,128]{4,3,2,1,0:T(8,128)} copy(f32[2,6,8,32,128]{4,3,2,1,0:T(8,128)S(1)} %pseudo_time_step.1) | data formatting | bytes 3145728

commit v3 on v2

--- a/solution.py
+++ b/solution.py
@@ -17,7 +17,7 @@
 LAYERS = 8
 ROWS = 32
 TILE = 8
-TAKE = 2
+TAKE = 3
 GROUPS = VARS // TAKE
 LANES = 128
 GROUP = 16
@@ -76,7 +76,7 @@
     q, dt_hbm, freq, jac_hbm, shift_hbm, out,
     cells, step, jac, shift, rows_out, rows_in, columns, ghosts,
     gathered, beyond, derived, returned, fresh,
-    local_sem, out_send, out_recv, back_send, back_recv, side_send, side_recv, swap_send, swap_recv,
+    local_sem, out_send, out_recv, back_send, back_recv, side_send, side_recv, swap_send, swap_recv, entered,
 ):
     me = lax.axis_index("inst")
     rad = lax.axis_index("rad")
@@ -95,10 +95,22 @@
     meets = jnp.logical_and(x == 1 - rad, c == 1 - rad)
 
     barrier = pltpu.get_barrier_semaphore()
-    for peer, _, _ in peers:
-        pl.semaphore_signal(barrier, inc=1, device_id={"inst": peer}, device_id_type=MESH)
-    for peer in (after, before, across):
-        pl.semaphore_signal(barrier, inc=1, device_id=peer, device_id_type=MESH)
+    for dx, dy in [(1, 2), (1, 1), (1, 3), (0, 2), (1, 0), (0, 1), (0, 3)]:
+        chip = lax.rem(x + dx, 2) * 4 + lax.rem(y + dy, 4)
+        pl.semaphore_signal(barrier, inc=1, device_id={"inst": 2 * chip}, device_id_type=MESH)
+
+    @pl.when(c == 1)
+    def _():
+        pl.semaphore_signal(barrier, inc=1, device_id={"inst": me - c}, device_id_type=MESH)
+
+    for axis, place, chip in (
+        ("circ", after["circ"], me // 2),
+        ("circ", before["circ"], me // 2),
+        ("rad", 1 - rad, (1 - x) * 4 + y),
+    ):
+        pl.semaphore_signal(
+            barrier, inc=1, device_id={axis: place, "inst": 2 * chip + 1}, device_id_type=MESH
+        )
 
     my_layer, my_row = x * 4 + c * 2, pl.multiple_of(y * TILE, TILE)
     loads = [
@@ -123,7 +135,15 @@
         )
     for copy in small:
         copy.start()
-    pl.semaphore_wait(barrier, GROUP - 1 + 3)
+
+    @pl.when(c == 0)
+    def _():
+        pl.semaphore_wait(barrier, GROUP - 1)
+        pl.semaphore_signal(entered, inc=1, device_id={"inst": me + 1 - c}, device_id_type=MESH)
+
+    @pl.when(c == 1)
+    def _():
+        pl.semaphore_wait(entered, 1)
 
     def send_out(k, _):
         slot, g = k // GROUPS, lax.rem(k, GROUPS)
@@ -174,6 +194,16 @@
             side_send.at[3], side_recv.at[3], device_id=before, device_id_type=MESH,
         ),
     ]
+
+    @pl.when(c == 1)
+    def _():
+        pl.semaphore_wait(barrier, 6)
+        pl.semaphore_signal(entered, inc=1, device_id={"inst": me - c}, device_id_type=MESH)
+
+    @pl.when(c == 0)
+    def _():
+        pl.semaphore_wait(entered, 1)
+
     for copy in side_copies:
         copy.start()
     cells[:, :, 0, PAD:PAD + ROWS] = jnp.zeros((2, VARS, ROWS, LANES), jnp.float32)
@@ -361,6 +391,7 @@
             pltpu.VMEM((2, VARS, LAYERS, ROWS, LANES), f32),
             dma((6,)), dma, dma((2 * GROUPS,)), dma, dma((2 * GROUPS,)),
             dma((4,)), dma((4,)), dma((GROUPS,)), dma((GROUPS,)),
+            pltpu.SemaphoreType.REGULAR,
         ],
         compiler_params=pltpu.CompilerParams(
             collective_id=0, has_side_effects=True, vmem_limit_bytes=40 << 20

time: 45.3 us -> 43.9 us (0.969)
  Pallas kernels: 43.4 us -> 41.9 us
    pallas_call x1, Pallas kernels: 43.4 us -> 41.9 us  [per_device(): pl.pallas_call(kernel, name='pseudo_time_step', out_shape=pltpu.VMEM(flow...]
where the time goes in v3:
time: 43.9 us; the launch traced here: 43.7 us
  Pallas kernels  41.9 us (95%)
  local copies, waits for them, and re-layouts  1.15 us (3%)
  between operations  0.66 us (2%)
    pallas_call x1, Pallas kernels, per_device(): pl.pallas_call(kernel, name='pseudo_time_step', out_shape=pltpu.VMEM(flow...  41.9 us
    unnamed x1, local copies, waits for them, and re-layouts  1.15 us

profile of v3, /device:TPU:1, one launch (start us, length us, event | category | flops | bytes accessed | tf_op | source)
XLA Modules:
  0.0 43.7 jit_solution(10802172965313621531)
XLA Ops:
  0.7 41.9 %pseudo_time_step.1 = f32[2,6,8,32,128]{4,3,2,1,0:T(8,128)S(1)} custom-call(f32[2,6,8,32,128]{4,3,2,1,0:T(8,128)} %q.1, f32[8,32,128]{2,1,0:T(8,128)} %dt_hbm.1, f32[1]{0:T(128)S(6)} %copy.8.freq, f32[3,6,6]{2,1,0:T(8,128)} %jac_hbm.1, s32[32]{0:T(128)} %shift_hbm.1), custom_call_target="tpu_custom_call" | custom-call | flops 40000000 | bytes 4000000 | tf_op jit(solution)/shard_map/pseudo_time_step/pallas_call | solution.py:372
  42.6 1.1 %copy.7 = f32[2,6,8,32,128]{4,3,2,1,0:T(8,128)} copy(f32[2,6,8,32,128]{4,3,2,1,0:T(8,128)S(1)} %pseudo_time_step.1) | data formatting | bytes 3145728

commit v4 on v3

--- a/solution.py
+++ b/solution.py
@@ -22,6 +22,7 @@
 LANES = 128
 GROUP = 16
 PAD = 8
+FIRST = 1
 
 
 def spectral_weights(length):
@@ -242,9 +243,26 @@
             beyond[m, u] = side * total - 0.5 * w[u]
         return 0
 
+    def which(k):
+        return lax.rem(k // GROUPS + meets.astype(jnp.int32), 2), lax.rem(k, GROUPS)
+
+    def post(k, early):
+        slot, g = which(k)
+        layer = my_layer + lax.rem(slot + 1 - rad, 2)
+        for peer, _, _ in peers:
+            enters_early = peer == FIRST
+
+            @pl.when(enters_early if early else jnp.logical_not(enters_early))
+            def _():
+                pltpu.make_async_remote_copy(
+                    derived.at[slot, pl.ds(2 * peer, 2), pl.ds(g * TAKE, TAKE)],
+                    returned.at[:, pl.ds(g * TAKE, TAKE), layer, pl.ds(my_row, TILE)],
+                    back_send, back_recv.at[slot * GROUPS + g],
+                    device_id={"inst": peer}, device_id_type=MESH,
+                ).start()
+
     def send_back(k, _):
-        slot = lax.rem(k // GROUPS + meets.astype(jnp.int32), 2)
-        g = lax.rem(k, GROUPS)
+        slot, g = which(k)
         meeting = jnp.logical_and(meets, slot == 0)
 
         @pl.when(jnp.logical_not(meeting))
@@ -271,20 +289,20 @@
                     derived[0, m, v] = derived[0, m, v] + beyond[m, v]
 
         layer = my_layer + lax.rem(slot + 1 - rad, 2)
-        for peer, _, _ in peers:
-            pltpu.make_async_remote_copy(
-                derived.at[slot, pl.ds(2 * peer, 2), pl.ds(g * TAKE, TAKE)],
-                returned.at[:, pl.ds(g * TAKE, TAKE), layer, pl.ds(my_row, TILE)],
-                back_send, back_recv.at[slot * GROUPS + g],
-                device_id={"inst": peer}, device_id_type=MESH,
-            ).start()
         for n in range(2):
             for i in range(TAKE):
                 v = g * TAKE + i
                 returned[n, v, layer, pl.ds(my_row, TILE)] = derived[slot, 2 * me + n, v]
+        post(k, True)
+
+        @pl.when(k > 0)
+        def _():
+            post(k - 1, False)
+
         return 0
 
     lax.fori_loop(0, 2 * GROUPS, send_back, 0)
+    post(2 * GROUPS - 1, False)
 
     for copy in side_copies:
         copy.wait_recv()

time: 43.9 us -> 43 us (0.979)
  Pallas kernels: 41.9 us -> 40.6 us
    pallas_call x1, Pallas kernels: 41.9 us -> 40.6 us  [per_device(): pl.pallas_call(kernel, name='pseudo_time_step', out_shape=pltpu.VMEM(flow...]
where the time goes in v4:
time: 43 us; the launch traced here: 42.4 us
  Pallas kernels  40.6 us (94%)
  local copies, waits for them, and re-layouts  1.15 us (3%)
  between operations  0.66 us (2%)
    pallas_call x1, Pallas kernels, per_device(): pl.pallas_call(kernel, name='pseudo_time_step', out_shape=pltpu.VMEM(flow...  40.6 us
    unnamed x1, local copies, waits for them, and re-layouts  1.15 us

profile of v4, /device:TPU:1, one launch (start us, length us, event | category | flops | bytes accessed | tf_op | source)
XLA Modules:
  0.0 42.4 jit_solution(16195685904770773324)
XLA Ops:
  0.7 40.6 %pseudo_time_step.1 = f32[2,6,8,32,128]{4,3,2,1,0:T(8,128)S(1)} custom-call(f32[2,6,8,32,128]{4,3,2,1,0:T(8,128)} %q.1, f32[8,32,128]{2,1,0:T(8,128)} %dt_hbm.1, f32[1]{0:T(128)S(6)} %copy.8.freq, f32[3,6,6]{2,1,0:T(8,128)} %jac_hbm.1, s32[32]{0:T(128)} %shift_hbm.1), custom_call_target="tpu_custom_call" | custom-call | flops 40000000 | bytes 4000000 | tf_op jit(solution)/shard_map/pseudo_time_step/pallas_call | solution.py:390
  41.3 1.1 %copy.7 = f32[2,6,8,32,128]{4,3,2,1,0:T(8,128)} copy(f32[2,6,8,32,128]{4,3,2,1,0:T(8,128)S(1)} %pseudo_time_step.1) | data formatting | bytes 3145728

commit v5 on v4

--- a/solution.py
+++ b/solution.py
@@ -22,7 +22,6 @@
 LANES = 128
 GROUP = 16
 PAD = 8
-FIRST = 1
 
 
 def spectral_weights(length):
@@ -250,7 +249,7 @@
         slot, g = which(k)
         layer = my_layer + lax.rem(slot + 1 - rad, 2)
         for peer, _, _ in peers:
-            enters_early = peer == FIRST
+            enters_early = lax.rem(peer, 2) == 1
 
             @pl.when(enters_early if early else jnp.logical_not(enters_early))
             def _():

time: 43 us -> 43 us (level)
  no operation moved by 1% of the time
where the time goes in v5:
time: 43 us; the launch traced here: 42.2 us
  Pallas kernels  40.4 us (94%)
  local copies, waits for them, and re-layouts  1.15 us (3%)
  between operations  0.66 us (2%)
    pallas_call x1, Pallas kernels, per_device(): pl.pallas_call(kernel, name='pseudo_time_step', out_shape=pltpu.VMEM(flow...  40.4 us
    unnamed x1, local copies, waits for them, and re-layouts  1.15 us

profile of v5, /device:TPU:1, one launch (start us, length us, event | category | flops | bytes accessed | tf_op | source)
XLA Modules:
  0.0 42.2 jit_solution(17146804735893548502)
XLA Ops:
  0.7 40.4 %pseudo_time_step.1 = f32[2,6,8,32,128]{4,3,2,1,0:T(8,128)S(1)} custom-call(f32[2,6,8,32,128]{4,3,2,1,0:T(8,128)} %q.1, f32[8,32,128]{2,1,0:T(8,128)} %dt_hbm.1, f32[1]{0:T(128)S(6)} %copy.8.freq, f32[3,6,6]{2,1,0:T(8,128)} %jac_hbm.1, s32[32]{0:T(128)} %shift_hbm.1), custom_call_target="tpu_custom_call" | custom-call | flops 40000000 | bytes 4000000 | tf_op jit(solution)/shard_map/pseudo_time_step/pallas_call | solution.py:389
  41.1 1.1 %copy.7 = f32[2,6,8,32,128]{4,3,2,1,0:T(8,128)} copy(f32[2,6,8,32,128]{4,3,2,1,0:T(8,128)S(1)} %pseudo_time_step.1) | data formatting | bytes 3145728

commit v6 on v5

--- a/solution.py
+++ b/solution.py
@@ -17,7 +17,7 @@
 LAYERS = 8
 ROWS = 32
 TILE = 8
-TAKE = 3
+TAKE = 2
 GROUPS = VARS // TAKE
 LANES = 128
 GROUP = 16

time: 43 us -> 43.1 us (level)
  the two profiles are of different devices: /device:TPU:1 before, /device:TPU:0 now
where the time goes in v6:
time: 43.1 us; the launch traced here: 43 us
  Pallas kernels  41.2 us (96%)
  local copies, waits for them, and re-layouts  1.15 us (3%)
  between operations  0.66 us (2%)
    pallas_call x1, Pallas kernels, per_device(): pl.pallas_call(kernel, name='pseudo_time_step', out_shape=pltpu.VMEM(flow...  41.2 us
    unnamed x1, local copies, waits for them, and re-layouts  1.15 us

profile of v6, /device:TPU:0, one launch (start us, length us, event | category | flops | bytes accessed | tf_op | source)
XLA Modules:
  0.0 43.0 jit_solution(11536647600204677965)
XLA Ops:
  0.7 41.2 %pseudo_time_step.1 = f32[2,6,8,32,128]{4,3,2,1,0:T(8,128)S(1)} custom-call(f32[2,6,8,32,128]{4,3,2,1,0:T(8,128)} %q.1, f32[8,32,128]{2,1,0:T(8,128)} %dt_hbm.1, f32[1]{0:T(128)S(6)} %copy.8.freq, f32[3,6,6]{2,1,0:T(8,128)} %jac_hbm.1, s32[32]{0:T(128)} %shift_hbm.1), custom_call_target="tpu_custom_call" | custom-call | flops 40000000 | bytes 4000000 | tf_op jit(solution)/shard_map/pseudo_time_step/pallas_call | solution.py:389
  41.8 1.1 %copy.7 = f32[2,6,8,32,128]{4,3,2,1,0:T(8,128)} copy(f32[2,6,8,32,128]{4,3,2,1,0:T(8,128)S(1)} %pseudo_time_step.1) | data formatting | bytes 3145728
